TPU v7x, 1024 devices: a whole 8x8x8 slice. The times are simulated.
1024 devices in a mesh: dp: 16 (over z, core), blk: 16 (over y_lo, x), pack: 4 (over y_hi).
Axes of the slice: x: 8, y: 8 (y_hi: 4, y_lo: 2; y = y_hi * 2 + y_lo), z: 8, core: 2. Of those that a mesh axis runs over, the one named last changes fastest.
Arguments:
- points: bfloat16 [1572864, 256], P(('dp', 'blk', 'pack')), may hold values from -6 to 6
- neighbours: int32 [27, 1572864], P(None, ('dp', 'blk', 'pack')), may hold values from 0 to 127, as said below
- tile_points: int32 [12288], P(('dp', 'blk', 'pack')), may hold values from 1 to 128
- tile_shape: int32 [12288], P(('dp', 'blk', 'pack')), may hold values from 0 to 6143, as said below
- captions: bfloat16 [6144, 1280], P(('dp', 'blk', 'pack')), may hold values from -6 to 6
- positive: int32 [6144], P(('dp', 'blk', 'pack')), may hold values from 0 to 95
- self_weight: bfloat16 [256, 256], replicated, may hold values from -0.375 to 0.375
- neighbour_weight: bfloat16 [256, 256], replicated, may hold values from -0.375 to 0.375
- projection: bfloat16 [256, 1280], replicated, may hold values from -0.375 to 0.375
- logit_scale: float32 [1], replicated, may hold values from 3 to 10
- logit_bias: float32 [1], replicated, may hold values from -4 to -1
Outputs:
- caption_grad: float32 [6144, 1280], P(('dp', 'blk', 'pack'))
- projection_grad: float32 [256, 1280], P('dp')
Inputs may be any that keep to these rules, and one draw needn't show every extreme that they name: `neighbours`: every entry of a point is below the tile_points of that point's tile. A tile's shape belongs to a device of the tile's own pack group: tile_shape // 6 // 4 equals the holding device's number // 4. Each device holds exactly one tile of each of its own 6 shapes, and at most 6 tiles of the shapes of any one other device. Every shape has a tile.
All inputs are finite; a program needn't handle non-finite values.
Results may differ from a plain program's by a relative error of at most 0.0044.
Values may be sent and summed in bfloat16 or wider, within the bound.
No kernel may reach another device: no remote copies, remote signals or barrier semaphores. Data moves between devices by JAX's collectives and lax.ppermute only.
A program may use at most 32 MiB of HBM per device.

v0:
```python
import jax
import jax.numpy as jnp
from jax import lax
from jax.experimental import pallas as pl
from jax.experimental.pallas import tpu as pltpu
from jax.sharding import PartitionSpec as P

NEIGH = 27
TILE_PTS = 128
SLOT = 8
ENCODE_VMEM = 60 * 1024 * 1024
F32 = jnp.float32
BF16 = jnp.bfloat16
DOT0 = (((0,), (0,)), ((), ()))
DOT1 = (((1,), (1,)), ((), ()))


def encode_kernel(
    owned,
    counts_far,
    shapes_far,
    points_far,
    links_far,
    self_far,
    neighbour_far,
    sums,
    counts,
    shapes,
    points,
    links,
    self_weight,
    neighbour_weight,
    arrived,
):
    copies = [
        pltpu.make_async_copy(far, near, arrived.at[i])
        for i, (far, near) in enumerate(
            (
                (links_far, links),
                (points_far, points),
                (self_far, self_weight),
                (neighbour_far, neighbour_weight),
                (counts_far, counts),
                (shapes_far, shapes),
            )
        )
    ]
    for copy in copies:
        copy.start()
    sums[...] = jnp.zeros_like(sums)
    tiles = points.shape[0] // TILE_PTS
    rows = lax.broadcasted_iota(jnp.int32, (TILE_PTS, TILE_PTS), 0).astype(F32).astype(BF16)
    ones = jnp.ones((TILE_PTS, TILE_PTS), BF16)
    zeros = jnp.zeros((TILE_PTS, TILE_PTS), BF16)
    copies[0].wait()
    adjacencies = []
    for tile in range(tiles):
        columns = links[:, tile * TILE_PTS : (tile + 1) * TILE_PTS].astype(F32)
        adjacency = zeros
        for k in range(NEIGH):
            link = jnp.broadcast_to(columns[k : k + 1, :], (16, TILE_PTS)).astype(BF16)
            link = jnp.concatenate([link] * (TILE_PTS // 16), axis=0)
            adjacency = adjacency + jnp.where(link == rows, ones, zeros)
        adjacencies.append(adjacency)
    for copy in copies[1:]:
        copy.wait()
    aggregates = []
    for tile in range(tiles):
        span = slice(tile * TILE_PTS, (tile + 1) * TILE_PTS)
        total = lax.dot_general(adjacencies[tile], points[span, :], DOT0, preferred_element_type=F32)
        aggregates.append((total * (1.0 / NEIGH)).astype(BF16))
    features = points[...]
    before = jnp.dot(features, self_weight[...], preferred_element_type=F32) + jnp.dot(
        jnp.concatenate(aggregates, axis=0), neighbour_weight[...], preferred_element_type=F32
    )
    center = before - jnp.mean(before, axis=-1, keepdims=True)
    spread = jnp.mean(center * center, axis=-1, keepdims=True)
    hidden = features.astype(F32) + jnp.maximum(center * lax.rsqrt(spread + 1e-05), 0.0)
    point = lax.broadcasted_iota(jnp.int32, (TILE_PTS, 1), 0)
    for tile in range(tiles):
        span = slice(tile * TILE_PTS, (tile + 1) * TILE_PTS)
        kept = jnp.where(point < counts[tile], hidden[span, :], 0.0)
        place = lax.rem(shapes[tile], sums.shape[0] // SLOT * owned)
        slot = pl.ds(lax.div(place, owned) * SLOT + lax.rem(place, owned), 1)
        sums[slot, :] = sums[slot, :] + jnp.sum(kept, axis=0, keepdims=True)


def encode(counts, shapes, points, links, self_weight, neighbour_weight, packs, owned):
    channels = points.shape[1]
    vmem = pl.BlockSpec(memory_space=pltpu.VMEM)
    far = pl.BlockSpec(memory_space=pl.ANY)

    def body(*refs):
        encode_kernel(owned, *refs)

    return pl.pallas_call(
        body,
        out_shape=jax.ShapeDtypeStruct((packs * SLOT, channels), F32),
        in_specs=[far] * 6,
        out_specs=vmem,
        scratch_shapes=[
            pltpu.SMEM(counts.shape, counts.dtype),
            pltpu.SMEM(shapes.shape, shapes.dtype),
            pltpu.VMEM(points.shape, points.dtype),
            pltpu.VMEM(links.shape, links.dtype),
            pltpu.VMEM(self_weight.shape, self_weight.dtype),
            pltpu.VMEM(neighbour_weight.shape, neighbour_weight.dtype),
            pltpu.SemaphoreType.DMA((6,)),
        ],
        compiler_params=pltpu.CompilerParams(vmem_limit_bytes=ENCODE_VMEM),
        name="encode",
    )(counts, shapes, points, links, self_weight, neighbour_weight)


def caption_kernel(owned, blks, positive, encoded, captions, projection, out):
    channels, width = projection.shape
    half = width // 2
    wide = captions[...].astype(F32)
    unit = wide / jnp.sqrt(jnp.sum(wide * wide, axis=-1, keepdims=True) + 1e-06)
    unit = jnp.concatenate([unit, jnp.zeros((SLOT - owned, width), F32)], axis=0).astype(BF16)
    mixed = lax.dot_general(unit, projection[...], DOT1, preferred_element_type=F32)
    level = jnp.mean(mixed, axis=-1, keepdims=True)
    mixed = mixed - level
    unit = unit.astype(F32)
    where = lax.axis_index("blk")
    lanes = lax.broadcasted_iota(jnp.int32, (1, out.shape[1]), 1) - owned // 2 * channels
    places = jnp.zeros(lanes.shape, F32)
    levels = jnp.zeros(lanes.shape, F32)
    for i in range(owned):
        place = positive[i]
        padded = lax.div(place, owned) * SLOT + lax.rem(place, owned)
        places = places + jnp.where(lanes == i, padded.astype(F32), 0.0)
        levels = levels + jnp.where(lanes == where * SLOT + i, level[i : i + 1, :], 0.0)
    for side in range(2):
        part = unit[0:owned, side * half : (side + 1) * half]
        rows = [jnp.concatenate([part, mixed[0:owned, :]], axis=1), places, levels]
        out[side * SLOT : (side + 1) * SLOT, :] = jnp.concatenate(rows, axis=0)


def caption_rows(positive, encoded, captions, projection, blks):
    owned, width = captions.shape
    channels = projection.shape[0]
    smem = pl.BlockSpec(memory_space=pltpu.SMEM)
    vmem = pl.BlockSpec(memory_space=pltpu.VMEM)

    def body(*refs):
        caption_kernel(owned, blks, *refs)

    return pl.pallas_call(
        body,
        out_shape=jax.ShapeDtypeStruct((2 * SLOT, width // 2 + channels), F32),
        in_specs=[smem, pl.BlockSpec(memory_space=pl.ANY), vmem, vmem],
        out_specs=vmem,
        compiler_params=pltpu.CompilerParams(vmem_limit_bytes=16 * 1024 * 1024),
        name="caption_rows",
    )(positive, encoded, captions, projection)


def pool_kernel(owned, blks, packs, scale, bias, sums, rows, out):
    channels = sums.shape[1]
    shape_sums = sums[0:SLOT, :]
    for p in range(1, packs):
        shape_sums = shape_sums + sums[p * SLOT : (p + 1) * SLOT, :]
    center = shape_sums - jnp.mean(shape_sums, axis=-1, keepdims=True)
    pooled = center * lax.rsqrt(jnp.mean(center * center, axis=-1, keepdims=True) + 1e-05)
    across = owned // 2
    spare = across * channels
    blocks = []
    for side in range(2):
        top = side * SLOT
        blocks.append(rows[top : top + owned, :])
        for line in range(2):
            held = [pooled[i : i + 1, :] for i in range(line * across, (line + 1) * across)]
            row = top + owned + line
            blocks.append(jnp.concatenate(held + [rows[row : row + 1, spare:]], axis=1))
    pair = jnp.concatenate(blocks, axis=0).astype(BF16)
    for j in range(0, blks * SLOT, 2 * SLOT):
        out[j : j + 2 * SLOT, :] = pair


def pool(scale, bias, sums, rows, owned, blks, packs):
    smem = pl.BlockSpec(memory_space=pltpu.SMEM)
    vmem = pl.BlockSpec(memory_space=pltpu.VMEM)

    def body(*refs):
        pool_kernel(owned, blks, packs, *refs)

    return pl.pallas_call(
        body,
        out_shape=jax.ShapeDtypeStruct((blks * SLOT, rows.shape[1]), BF16),
        in_specs=[smem, smem, vmem, vmem],
        out_specs=vmem,
        compiler_params=pltpu.CompilerParams(vmem_limit_bytes=16 * 1024 * 1024),
        name="pool",
    )(scale, bias, sums, rows)


def loss_kernel(owned, dps, blks, scale, bias, group_rows, projection, caption_grad, rows_grad):
    where = lax.axis_index("blk")
    group = blks * SLOT
    channels, width = projection.shape
    half = width // 2
    across = owned // 2
    given = group_rows[...]
    wanted = lax.broadcasted_iota(jnp.int32, (2 * blks, group), 0)
    wanted = lax.rem(wanted, blks) * SLOT + owned + lax.div(wanted, blks)
    lanes = lax.broadcasted_iota(jnp.int32, (2 * blks, group), 1)
    picked = jnp.dot(
        jnp.where(wanted == lanes, 1.0, 0.0).astype(BF16), given, preferred_element_type=F32
    )
    pooled = jnp.concatenate(
        [
            picked[side * blks : (side + 1) * blks, i * channels : (i + 1) * channels]
            for side in range(2)
            for i in range(across)
        ],
        axis=0,
    ).astype(BF16)
    places = across * channels
    positive = jnp.concatenate(
        [picked[0:blks, places + i : places + i + 1] for i in range(owned)], axis=0
    ).astype(jnp.int32)
    raw_embed = jnp.dot(pooled, projection[...], preferred_element_type=F32)
    norms = jnp.sqrt(jnp.sum(raw_embed * raw_embed, axis=-1, keepdims=True) + 1e-06)
    unit_shape = raw_embed / norms
    shape_embed = unit_shape.astype(BF16)
    dots = lax.dot_general(pooled, given[:, half : half + channels], DOT1, preferred_element_type=F32)
    levels = jnp.sum(picked[blks : 2 * blks, places : places + group], axis=0, keepdims=True)
    dots = (dots + levels * jnp.sum(pooled.astype(F32), axis=-1, keepdims=True)) / norms
    logits = scale[0] * dots + bias[0]
    columns = lax.broadcasted_iota(jnp.int32, logits.shape, 1)
    label = jnp.where(columns == positive, 1.0, -1.0)
    coef = -label * jax.nn.sigmoid(-label * logits)
    coef = jnp.where(lax.rem(columns, SLOT) < owned, coef, 0.0).astype(BF16)
    mine = lax.broadcasted_iota(jnp.int32, (SLOT, group), 0) + where * SLOT
    pick = jnp.where(mine == lax.broadcasted_iota(jnp.int32, (SLOT, group), 1), 1.0, 0.0).astype(BF16)
    own_coef = lax.dot_general(pick, coef, DOT1, preferred_element_type=F32).astype(BF16)
    caption_grad[...] = scale[0] * jnp.dot(own_coef, shape_embed, preferred_element_type=F32)
    shape_grad = scale[0] * jnp.dot(coef, given[:, 0:half], preferred_element_type=F32)
    along = scale[0] * jnp.sum(coef.astype(F32) * dots, axis=-1, keepdims=True)
    side = lax.rem(where, 2)
    unit_half = jnp.where(side == 0, unit_shape[:, 0:half], unit_shape[:, half:width])
    raw_grad = (shape_grad - unit_half * along) / norms
    each = rows_grad.shape[1]
    kept = lax.broadcasted_iota(jnp.int32, (dps * each, channels), 0)
    chosen = lax.div(kept, each) * (channels // dps) + lax.rem(kept, each) + lax.div(where, 2) * each
    select = jnp.where(
        chosen == lax.broadcasted_iota(jnp.int32, (dps * each, channels), 1), 1.0, 0.0
    ).astype(BF16)
    factors = lax.dot_general(select, pooled, DOT1, preferred_element_type=F32).astype(BF16)
    high = raw_grad.astype(BF16)
    low = (raw_grad - high.astype(F32)).astype(BF16)
    rows = jnp.dot(factors, high, preferred_element_type=F32) + jnp.dot(
        factors, low, preferred_element_type=F32
    )
    rows_grad[...] = rows.reshape(rows_grad.shape)


def loss_grads(scale, bias, group_rows, projection, owned, dps, blks):
    channels, width = projection.shape
    smem = pl.BlockSpec(memory_space=pltpu.SMEM)
    vmem = pl.BlockSpec(memory_space=pltpu.VMEM)

    def body(*refs):
        loss_kernel(owned, dps, blks, *refs)

    return pl.pallas_call(
        body,
        out_shape=(
            jax.ShapeDtypeStruct((SLOT, width), F32),
            jax.ShapeDtypeStruct((dps, 2 * channels // dps // blks, width // 2), F32),
        ),
        in_specs=[smem, smem, vmem, vmem],
        out_specs=(vmem, vmem),
        compiler_params=pltpu.CompilerParams(vmem_limit_bytes=32 * 1024 * 1024),
        name="loss_grads",
    )(scale, bias, group_rows, projection)


def spread_row(parts, copies):
    sources, each, half = parts.shape

    def body(arrived, out):
        total = arrived[0]
        for d in range(1, sources):
            total = total + arrived[d]
        out[...] = jnp.broadcast_to(total.astype(BF16)[None], out.shape)

    vmem = pl.BlockSpec(memory_space=pltpu.VMEM)
    return pl.pallas_call(
        body,
        out_shape=jax.ShapeDtypeStruct((copies, each, half), BF16),
        in_specs=[vmem],
        out_specs=vmem,
        compiler_params=pltpu.CompilerParams(vmem_limit_bytes=8 * 1024 * 1024),
        name="spread_row",
    )(parts)


def finish(every, caption_grad, packs, owned):
    places, each, half = every.shape

    def body(parts, grad, out, grad_out):
        grad_out[...] = grad[0:owned, :]
        for b in range(places // packs):
            total = parts[b * packs].astype(F32)
            for p in range(1, packs):
                total = total + parts[b * packs + p].astype(F32)
            row, side = b // 2, b % 2
            out[row * each : (row + 1) * each, side * half : (side + 1) * half] = total

    vmem = pl.BlockSpec(memory_space=pltpu.VMEM)
    return pl.pallas_call(
        body,
        out_shape=(
            jax.ShapeDtypeStruct((places // packs // 2 * each, 2 * half), F32),
            jax.ShapeDtypeStruct((owned, 2 * half), F32),
        ),
        in_specs=[vmem, vmem],
        out_specs=(vmem, vmem),
        compiler_params=pltpu.CompilerParams(vmem_limit_bytes=8 * 1024 * 1024),
        name="finish",
    )(every, caption_grad)


def exchange(array, axes, size):
    blocks = array.reshape(size, array.shape[0] // size, array.shape[1])
    return lax.all_to_all(blocks, axes, 0, 0, tiled=True).reshape(array.shape)


def shards(
    points,
    neighbours,
    tile_points,
    tile_shape,
    captions,
    positive,
    self_weight,
    neighbour_weight,
    projection,
    logit_scale,
    logit_bias,
):
    owned = captions.shape[0]
    packs = lax.axis_size("pack")
    blks = lax.axis_size("blk")
    dps = lax.axis_size("dp")
    sums = encode(
        tile_points,
        tile_shape,
        points,
        neighbours,
        self_weight,
        neighbour_weight,
        packs,
        owned,
    )
    rows = caption_rows(positive, sums, captions, projection, blks)
    sums = exchange(sums, "pack", packs)
    group_rows = exchange(pool(logit_scale, logit_bias, sums, rows, owned, blks, packs), "blk", blks)
    caption_grad, rows_grad = loss_grads(
        logit_scale,
        logit_bias,
        group_rows,
        projection,
        owned,
        dps,
        blks,
    )
    rows_grad = lax.all_to_all(rows_grad, "dp", 0, 0, tiled=True)
    row = spread_row(rows_grad, blks * packs)
    every = lax.all_to_all(row, ("blk", "pack"), 0, 0, tiled=True)
    projection_grad, caption_grad = finish(every, caption_grad, packs, owned)
    return (caption_grad, projection_grad)


def solution(mesh):
    in_specs = (
        P(("dp", "blk", "pack"), None),
        P(None, ("dp", "blk", "pack")),
        P(("dp", "blk", "pack")),
        P(("dp", "blk", "pack")),
        P(("dp", "blk", "pack"), None),
        P(("dp", "blk", "pack")),
        P(),
        P(),
        P(),
        P(),
        P(),
    )
    out_specs = (P(("dp", "blk", "pack"), None), P("dp", None))
    return jax.shard_map(shards, mesh=mesh, in_specs=in_specs, out_specs=out_specs, check_vma=False)
```

profile of v0, /device:TPU:2, one launch (start us, length us, event | category | flops | bytes accessed | tf_op | source)
XLA Modules:
  0.0 79.9 jit_solution(2513678994790363470)
XLA Ops:
  0.6 0.0 copy-start
  0.6 4.0 %encode.1.refs_1_ = f32[32,256]{1,0:T(8,128)} custom-call(s32[12]{0:T(128)} %refs_0_.4, s32[12]{0:T(128)} %refs_1_.3, bf16[1536,256]{1,0:T(8,128)(2,1)} %refs_2_.2, s32[27,1536]{1,0:T(8,128)} %refs_3_.3, bf16[256,256]{1,0:T(8,128)(2,1)} %refs_4_.1, bf16[256,256]{1,0:T(8,128)(2,1)} %refs_5_.1), custom_call_target="tpu_custom_call" | custom-call | tf_op jit(solution)/shard_map/encode/pallas_call | solution.py:96
  4.7 0.0 copy-start.1
  4.7 0.0 copy-start.2
  4.7 7.6 %all-to-all-start = ((f32[4,8,256]{2,1,0:T(8,128)}), f32[4,8,256]{2,1,0:T(8,128)S(1)}, u32[]{:S(2)}, u32[]{:S(2)}) async-start(f32[4,8,256]{2,1,0:T(8,128)} %bitcast.6), calls=%async_computation | async-start | bytes 65536 | tf_op jit(solution)/shard_map/all_to_all | solution.py:328
  12.9 0.0 copy-start.3
  13.6 0.0 copy-done
  13.6 0.0 copy-done.1
  13.6 0.0 copy-done.2
  13.6 0.0 copy-done.3
  13.6 1.0 %caption_rows.1.refs_3_ = f32[16,896]{1,0:T(8,128)S(1)} custom-call(s32[6]{0:T(128)S(1)} %copy-done.3, f32[32,256]{1,0:T(8,128)S(1)} %copy-done.1, bf16[6,1280]{1,0:T(8,128)(2,1)S(1)} %copy-done.2, bf16[256,1280]{1,0:T(8,128)(2,1)S(1)} %copy-done), custom_call_target="tpu_custom_call" | custom-call | tf_op jit(solution)/shard_map/caption_rows/pallas_call | solution.py:149
  14.6 5.5 %all-to-all-done = f32[4,8,256]{2,1,0:T(8,128)S(1)} async-done(((f32[4,8,256]{2,1,0:T(8,128)}), f32[4,8,256]{2,1,0:T(8,128)S(1)}, u32[]{:S(2)}, u32[]{:S(2)}) %all-to-all-start) | async-done | bytes 32800 | tf_op jit(solution)/shard_map/all_to_all | solution.py:328
  20.1 0.2 pool.1
  20.3 20.2 %all_to_all.20 = bf16[16,8,896]{2,1,0:T(8,128)(2,1)S(1)} all-to-all(bf16[16,8,896]{2,1,0:T(8,128)(2,1)S(1)} %bitcast.4), channel_id=1, replica_groups=mesh['dp'=16,'blk'=16,'pack'=4] {'blk'}, dimensions={0} | all-to-all | bytes 458752 | tf_op jit(solution)/shard_map/all_to_all | solution.py:328
  40.5 1.0 %loss_grads.1 = (f32[8,1280]{1,0:T(8,128)S(1)}, f32[16,2,640]{2,1,0:T(2,128)S(1)}) custom-call(f32[1]{0:T(128)S(6)} %copy.13.refs_0_, f32[1]{0:T(128)S(6)} %copy.14.refs_1_, bf16[128,896]{1,0:T(8,128)(2,1)S(1)} %bitcast.5, bf16[256,1280]{1,0:T(8,128)(2,1)S(1)} %copy-done), custom_call_target="tpu_custom_call" | custom-call | tf_op jit(solution)/shard_map/loss_grads/pallas_call | solution.py:267
  41.5 20.5 %all_to_all.21.arrived = f32[16,2,640]{2,1,0:T(2,128)S(1)} all-to-all(f32[16,2,640]{2,1,0:T(2,128)S(1)} %get-tuple-element.6), channel_id=1, replica_groups=mesh['dp'=16,'blk'=16,'pack'=4] {'dp'}, dimensions={0} | all-to-all | bytes 163840 | tf_op jit(solution)/shard_map/all_to_all | solution.py:370
  62.0 17.2 %all_to_all.22.parts = bf16[64,2,640]{2,1,0:T(2,128)(2,1)S(1)} all-to-all(bf16[64,2,640]{2,1,0:T(2,128)(2,1)S(1)} %spread_row.1), channel_id=1, replica_groups=mesh['dp'=16,'blk'=16,'pack'=4] {'blk','pack'}, dimensions={0} | all-to-all | bytes 327680 | tf_op jit(solution)/shard_map/all_to_all | solution.py:372
  79.2 0.7 finish.1
  (1 shorter events, 0.0 us)
Async XLA Ops:
  0.6 12.9 %copy-start = (bf16[256,1280]{1,0:T(8,128)(2,1)S(1)}, bf16[256,1280]{1,0:T(8,128)(2,1)}, u32[]{:S(2)}) copy-start(bf16[256,1280]{1,0:T(8,128)(2,1)} %refs_3_.5) | copy-start | bytes 1966084
  4.7 8.9 %copy-start.1 = (f32[32,256]{1,0:T(8,128)S(1)}, f32[32,256]{1,0:T(8,128)}, u32[]{:S(2)}) copy-start(f32[32,256]{1,0:T(8,128)} %encode.1.refs_1_) | copy-start | bytes 98308
  4.7 8.9 %copy-start.2 = (bf16[6,1280]{1,0:T(8,128)(2,1)S(1)}, bf16[6,1280]{1,0:T(8,128)(2,1)}, u32[]{:S(2)}) copy-start(bf16[6,1280]{1,0:T(8,128)(2,1)} %refs_2_.3) | copy-start | bytes 46084
  4.7 15.4 %all-to-all-start = ((f32[4,8,256]{2,1,0:T(8,128)}), f32[4,8,256]{2,1,0:T(8,128)S(1)}, u32[]{:S(2)}, u32[]{:S(2)}) async-start(f32[4,8,256]{2,1,0:T(8,128)} %bitcast.6), calls=%async_computation | async-start | bytes 65536 | tf_op jit(solution)/shard_map/all_to_all | solution.py:328
  12.9 0.7 copy-start.3
where the time goes:
time: 80.3 us; the launch traced here: 79.9 us
  blocking collectives  57.8 us (72%)
  starting transfers between devices  7.56 us (9%)
  Pallas kernels  6.91 us (9%)
  waiting for transfers between devices  5.5 us (7%)
  between operations  2.04 us (3%)
    all_to_all x1, blocking collectives, shards(): rows_grad = lax.all_to_all(rows_grad, 'dp', 0, 0, tiled=True)  20.5 us
    all_to_all x1, blocking collectives, exchange(): return lax.all_to_all(blocks, axes, 0, 0, tiled=True).reshape(array.shape)  20.2 us
    all_to_all x1, blocking collectives, shards(): every = lax.all_to_all(row, ('blk', 'pack'), 0, 0, tiled=True)  17.2 us
    all_to_all x1, starting transfers between devices, exchange(): return lax.all_to_all(blocks, axes, 0, 0, tiled=True).reshape(array.shape)  7.56 us
    all_to_all x1, waiting for transfers between devices, exchange(): return lax.all_to_all(blocks, axes, 0, 0, tiled=True).reshape(array.shape)  5.5 us
    pallas_call x1, Pallas kernels, encode(): pl.pallas_call(body, out_shape=jax.ShapeDtypeStruct((packs * SLOT, channe...  4 us
  transfers between devices with their start and end apart: 1, of which 1 were waited for; matrix products, arithmetic and copies ran while one was open for 0% of the time, Pallas kernels for 1%

commit v1 on v0

--- a/solution.py
+++ b/solution.py
@@ -253,7 +253,7 @@
     rows = jnp.dot(factors, high, preferred_element_type=F32) + jnp.dot(
         factors, low, preferred_element_type=F32
     )
-    rows_grad[...] = rows.reshape(rows_grad.shape)
+    rows_grad[...] = rows.reshape(rows_grad.shape).astype(BF16)
 
 
 def loss_grads(scale, bias, group_rows, projection, owned, dps, blks):
@@ -268,7 +268,7 @@
         body,
         out_shape=(
             jax.ShapeDtypeStruct((SLOT, width), F32),
-            jax.ShapeDtypeStruct((dps, 2 * channels // dps // blks, width // 2), F32),
+            jax.ShapeDtypeStruct((dps, 2 * channels // dps // blks, width // 2), BF16),
         ),
         in_specs=[smem, smem, vmem, vmem],
         out_specs=(vmem, vmem),
@@ -281,9 +281,9 @@
     sources, each, half = parts.shape
 
     def body(arrived, out):
-        total = arrived[0]
+        total = arrived[0].astype(F32)
         for d in range(1, sources):
-            total = total + arrived[d]
+            total = total + arrived[d].astype(F32)
         out[...] = jnp.broadcast_to(total.astype(BF16)[None], out.shape)
 
     vmem = pl.BlockSpec(memory_space=pltpu.VMEM)

time: 80.3 us -> 79.6 us (level)
  no operation moved by 1% of the time
where the time goes in v1:
time: 79.6 us; the launch traced here: 79.2 us
  blocking collectives  57.1 us (72%)
  starting transfers between devices  7.56 us (9%)
  Pallas kernels  6.93 us (9%)
  waiting for transfers between devices  5.5 us (7%)
  between operations  2.04 us (3%)
    all_to_all x1, blocking collectives, exchange(): return lax.all_to_all(blocks, axes, 0, 0, tiled=True).reshape(array.shape)  20.2 us
    all_to_all x1, blocking collectives, shards(): rows_grad = lax.all_to_all(rows_grad, 'dp', 0, 0, tiled=True)  20.1 us
    all_to_all x1, blocking collectives, shards(): every = lax.all_to_all(row, ('blk', 'pack'), 0, 0, tiled=True)  16.8 us
    all_to_all x1, starting transfers between devices, exchange(): return lax.all_to_all(blocks, axes, 0, 0, tiled=True).reshape(array.shape)  7.56 us
    all_to_all x1, waiting for transfers between devices, exchange(): return lax.all_to_all(blocks, axes, 0, 0, tiled=True).reshape(array.shape)  5.5 us
    pallas_call x1, Pallas kernels, encode(): pl.pallas_call(body, out_shape=jax.ShapeDtypeStruct((packs * SLOT, channe...  4 us
  transfers between devices with their start and end apart: 1, of which 1 were waited for; matrix products, arithmetic and copies ran while one was open for 0% of the time, Pallas kernels for 1%

profile of v1, /device:TPU:2, one launch (start us, length us, event | category | flops | bytes accessed | tf_op | source)
XLA Modules:
  0.0 79.2 jit_solution(15630878606255618085)
XLA Ops:
  0.6 0.0 copy-start
  0.6 4.0 %encode.1.refs_1_ = f32[32,256]{1,0:T(8,128)} custom-call(s32[12]{0:T(128)} %refs_0_.4, s32[12]{0:T(128)} %refs_1_.3, bf16[1536,256]{1,0:T(8,128)(2,1)} %refs_2_.2, s32[27,1536]{1,0:T(8,128)} %refs_3_.3, bf16[256,256]{1,0:T(8,128)(2,1)} %refs_4_.1, bf16[256,256]{1,0:T(8,128)(2,1)} %refs_5_.1), custom_call_target="tpu_custom_call" | custom-call | tf_op jit(solution)/shard_map/encode/pallas_call | solution.py:96
  4.7 0.0 copy-start.1
  4.7 0.0 copy-start.2
  4.7 7.6 %all-to-all-start = ((f32[4,8,256]{2,1,0:T(8,128)}), f32[4,8,256]{2,1,0:T(8,128)S(1)}, u32[]{:S(2)}, u32[]{:S(2)}) async-start(f32[4,8,256]{2,1,0:T(8,128)} %bitcast.6), calls=%async_computation | async-start | bytes 65536 | tf_op jit(solution)/shard_map/all_to_all | solution.py:328
  12.9 0.0 copy-start.3
  13.6 0.0 copy-done
  13.6 0.0 copy-done.1
  13.6 0.0 copy-done.2
  13.6 0.0 copy-done.3
  13.6 1.0 %caption_rows.1.refs_3_ = f32[16,896]{1,0:T(8,128)S(1)} custom-call(s32[6]{0:T(128)S(1)} %copy-done.3, f32[32,256]{1,0:T(8,128)S(1)} %copy-done.1, bf16[6,1280]{1,0:T(8,128)(2,1)S(1)} %copy-done.2, bf16[256,1280]{1,0:T(8,128)(2,1)S(1)} %copy-done), custom_call_target="tpu_custom_call" | custom-call | tf_op jit(solution)/shard_map/caption_rows/pallas_call | solution.py:149
  14.6 5.5 %all-to-all-done = f32[4,8,256]{2,1,0:T(8,128)S(1)} async-done(((f32[4,8,256]{2,1,0:T(8,128)}), f32[4,8,256]{2,1,0:T(8,128)S(1)}, u32[]{:S(2)}, u32[]{:S(2)}) %all-to-all-start) | async-done | bytes 32800 | tf_op jit(solution)/shard_map/all_to_all | solution.py:328
  20.1 0.2 pool.1
  20.3 20.2 %all_to_all.20 = bf16[16,8,896]{2,1,0:T(8,128)(2,1)S(1)} all-to-all(bf16[16,8,896]{2,1,0:T(8,128)(2,1)S(1)} %bitcast.4), channel_id=1, replica_groups=mesh['dp'=16,'blk'=16,'pack'=4] {'blk'}, dimensions={0} | all-to-all | bytes 458752 | tf_op jit(solution)/shard_map/all_to_all | solution.py:328
  40.5 1.0 %loss_grads.1 = (f32[8,1280]{1,0:T(8,128)S(1)}, bf16[16,2,640]{2,1,0:T(2,128)(2,1)S(1)}) custom-call(f32[1]{0:T(128)S(6)} %copy.13.refs_0_, f32[1]{0:T(128)S(6)} %copy.14.refs_1_, bf16[128,896]{1,0:T(8,128)(2,1)S(1)} %bitcast.5, bf16[256,1280]{1,0:T(8,128)(2,1)S(1)} %copy-done), custom_call_target="tpu_custom_call" | custom-call | tf_op jit(solution)/shard_map/loss_grads/pallas_call | solution.py:267
  41.5 20.1 %all_to_all.21.arrived = bf16[16,2,640]{2,1,0:T(2,128)(2,1)S(1)} all-to-all(bf16[16,2,640]{2,1,0:T(2,128)(2,1)S(1)} %get-tuple-element.6), channel_id=1, replica_groups=mesh['dp'=16,'blk'=16,'pack'=4] {'dp'}, dimensions={0} | all-to-all | bytes 81920 | tf_op jit(solution)/shard_map/all_to_all | solution.py:370
  61.6 16.8 %all_to_all.22.parts = bf16[64,2,640]{2,1,0:T(2,128)(2,1)S(1)} all-to-all(bf16[64,2,640]{2,1,0:T(2,128)(2,1)S(1)} %spread_row.1), channel_id=1, replica_groups=mesh['dp'=16,'blk'=16,'pack'=4] {'blk','pack'}, dimensions={0} | all-to-all | bytes 327680 | tf_op jit(solution)/shard_map/all_to_all | solution.py:372
  78.5 0.7 finish.1
  (1 shorter events, 0.0 us)
Async XLA Ops:
  0.6 12.9 %copy-start = (bf16[256,1280]{1,0:T(8,128)(2,1)S(1)}, bf16[256,1280]{1,0:T(8,128)(2,1)}, u32[]{:S(2)}) copy-start(bf16[256,1280]{1,0:T(8,128)(2,1)} %refs_3_.5) | copy-start | bytes 1966084
  4.7 8.9 %copy-start.1 = (f32[32,256]{1,0:T(8,128)S(1)}, f32[32,256]{1,0:T(8,128)}, u32[]{:S(2)}) copy-start(f32[32,256]{1,0:T(8,128)} %encode.1.refs_1_) | copy-start | bytes 98308
  4.7 8.9 %copy-start.2 = (bf16[6,1280]{1,0:T(8,128)(2,1)S(1)}, bf16[6,1280]{1,0:T(8,128)(2,1)}, u32[]{:S(2)}) copy-start(bf16[6,1280]{1,0:T(8,128)(2,1)} %refs_2_.3) | copy-start | bytes 46084
  4.7 15.4 %all-to-all-start = ((f32[4,8,256]{2,1,0:T(8,128)}), f32[4,8,256]{2,1,0:T(8,128)S(1)}, u32[]{:S(2)}, u32[]{:S(2)}) async-start(f32[4,8,256]{2,1,0:T(8,128)} %bitcast.6), calls=%async_computation | async-start | bytes 65536 | tf_op jit(solution)/shard_map/all_to_all | solution.py:328
  12.9 0.7 copy-start.3
